TPU v7x, 32 devices: a whole 2x2x4 slice. The times are simulated.
32 devices in a mesh: amp: 8 (over z, core), int: 4 (over y, x).
Axes of the slice: x: 2, y: 2, z: 4, core: 2. Of those that a mesh axis runs over, the one named last changes fastest.
Arguments:
- amps: bfloat16 [64, 4, 1000], P('amp', 'int'), may hold values from -6 to 6
- integrals: bfloat16 [8192, 4, 1000], P('amp', 'int'), may hold values from -0.25 to 0.25
- irrep_sizes: int32 [8], replicated, may hold values from 1 to 200, 1000 in all
- c_irreps: int32 [4], P('int'), may hold values from 0 to 7
Outputs:
- ladder: float32 [64, 8192], P('int', 'amp')
Inputs may be any that keep to these rules, and one draw needn't show every extreme that they name: `irrep_sizes`: the sizes sum to 1000 and the largest is exactly 200.
All inputs are finite; a program needn't handle non-finite values.
Results may differ from a plain program's by a relative error of at most 0.0003.
Values may be sent and summed in bfloat16 or wider, within the bound.
A program may use at most 64 MiB of HBM per device.

v0:
```python
import jax
import jax.numpy as jnp
from jax import lax
from jax.sharding import PartitionSpec as P


def body(amps, integrals, irrep_sizes, c_irreps):
    c_local = amps.shape[1]
    width = amps.shape[2]
    ab_local = integrals.shape[0]
    ends = jnp.cumsum(irrep_sizes)
    column = jnp.arange(width, dtype=jnp.int32)
    d_irrep = jnp.sum((column[:, None] >= ends[None, :]).astype(jnp.int32), axis=1)
    allowed = (d_irrep[None, :] == c_irreps[:, None]).astype(jnp.bfloat16)
    blocked = amps * allowed[None, :, :]
    flat_ints = integrals.reshape(ab_local, c_local * width)
    piece = lax.all_gather(blocked, "amp", axis=0, tiled=True)
    rows = piece.reshape(piece.shape[0], c_local * width)
    partial_sums = lax.dot_general(
        rows, flat_ints, (((1,), (1,)), ((), ())), preferred_element_type=jnp.float32
    )
    ladder = lax.psum_scatter(partial_sums, "int", scatter_dimension=0, tiled=True)
    return ladder


def solution(mesh):
    placed = (P("amp", "int", None), P("amp", "int", None), P(), P("int"))
    return jax.shard_map(
        body, mesh=mesh, in_specs=placed, out_specs=P("int", "amp"), check_vma=False
    )
```

profile of v0, /device:TPU:0, one launch (start us, length us, event | category | flops | bytes accessed | tf_op | source)
XLA Modules:
  0.0 58.0 jit_solution(16601213272534279916)
XLA Ops:
  6.5 0.0 copy-start
  6.5 0.0 reduce-scatter.2.cloned.1.call-start
  7.3 0.8 %reduce-window.8 = s32[8,1]{0,1:T(1,128)S(1)} reduce-window(s32[8,1]{0,1:T(1,128)} %bitcast.11, s32[]{:T(128)} %constant.4.clone.1), window={size=8x1 pad=7_0x0_0}, to_apply=%region_0.0 | reduce-window | flops 56 | bytes 68 | tf_op jit(solution)/shard_map/reduce-window.3
  8.2 0.1 convert_reduce_fusion
  8.3 0.7 %broadcast_multiply_fusion = bf16[8,1,1000]{2,0,1:T(8,128)(2,1)S(1)} fusion(bf16[8,1,1000]{2,0,1:T(8,128)(2,1)} %param.4, bf16[1000]{0:T(1024)(128)(2,1)S(1)} %compare_convert_fusion), kind=kLoop, calls=%fused_computation.5 | loop fusion | flops 8000 | bytes 34000 | tf_op jit(solution)/shard_map/mul | solution.py:15
  9.0 15.7 %all_gather.3 = bf16[64,1,1000]{2,0,1:T(8,128)(2,1)S(1)} all-gather(bf16[8,1,1000]{2,0,1:T(8,128)(2,1)S(1)} %broadcast_multiply_fusion), channel_id=1, replica_groups=mesh['amp'=8,'int'=4] {'amp'}, dimensions={0}, use_global_device_ids=true | all-gather | bytes 144000 | tf_op jit(solution)/shard_map/all_gather | solution.py:17
  24.7 0.0 copy-done
  24.7 1.3 %fusion = f32[64,1024]{1,0:T(8,128)} fusion(bf16[1024,1,1000]{0,2,1:T(8,128)(2,1)S(1)} %copy-done, bf16[64,1,1000]{2,0,1:T(8,128)(2,1)S(1)} %all_gather.3), kind=kOutput, calls=%fused_computation | convolution fusion | flops 131072000 | bytes 2438144 | tf_op jit(solution)/shard_map/dot_general | solution.py:19
  25.9 0.0 reduce-scatter.2.cloned.1.call-update
  26.0 25.2 %reduce-scatter.2.cloned.1.call-done = f32[16,1024]{1,0:T(8,128)} async-done(((f32[64,1024]{1,0:T(8,128)}), f32[16,1024]{1,0:T(8,128)}) %reduce-scatter.2.cloned.1.call-update) | async-done | bytes 65552 | tf_op jit(solution)/shard_map/reduce_scatter | solution.py:22
  (1 shorter events, 0.0 us)
Async XLA Ops:
  6.5 18.2 %copy-start = (bf16[1024,1,1000]{0,2,1:T(8,128)(2,1)S(1)}, bf16[1024,1,1000]{0,2,1:T(8,128)(2,1)}, u32[]{:S(2)}) copy-start(bf16[1024,1,1000]{0,2,1:T(8,128)(2,1)} %param.5) | copy-start | bytes 6144004
  6.5 44.7 %reduce-scatter.2.cloned.1.call-start = ((), (), s32[]{:S(2)}) async-start(), calls=%async_computation.1 | async-start | bytes 327680 | tf_op jit(solution)/shard_map/reduce_scatter | solution.py:22
Sparse Core Ops, SparseCore 0:
  26.1 25.0 reduce-scatter.1
where the time goes:
time: 58.3 us; the launch traced here: 58 us
  waiting for transfers between devices  25.2 us (43%)
  blocking collectives  15.7 us (27%)
  between operations  14.2 us (24%)
  other arithmetic  1.65 us (3%)
  matrix products  1.25 us (2%)
    reduce_scatter x1, waiting for transfers between devices, body(): lax.psum_scatter(partial_sums, 'int', scatter_dimension=0, tiled=True)  25.2 us
    all_gather x1, blocking collectives, body(): piece = lax.all_gather(blocked, 'amp', axis=0, tiled=True)  15.7 us
    dot_general x1, matrix products, body(): lax.dot_general(rows, flat_ints, (((1,), (1,)), ((), ())), preferred_elem...  1.25 us
  transfers between devices with their start and end apart: 1, of which 1 were waited for; matrix products, arithmetic and copies ran while one was open for 0% of the time, Pallas kernels for 0%

commit v1 on v0

v1 whole, which is shorter than its diff:
```python
import functools

import jax
import jax.numpy as jnp
from jax import lax
from jax.experimental import pallas as pl
from jax.experimental.pallas import tpu as pltpu
from jax.sharding import PartitionSpec as P

MESH = pl.DeviceIdType.MESH
MOST = 200
TILE = 16
LANES = 128


def window_of(width):
    return width


def chunks_of(columns):
    return 4 if columns % (4 * LANES) == 0 else 1


def kernel(n_amp, n_int, sizes_hbm, irreps_hbm, amps_hbm, ints_hbm, out_ref, sizes, irreps, amps, ints, packed, gathered, part, landed,
           local_sem, g_send, g_recv, r_send, r_recv):
    me_a, me_i = lax.axis_index("amp"), lax.axis_index("int")
    c_local, rows, width = amps.shape
    columns = ints.shape[2]
    chunks, _, out_rows, chunk = part.shape
    win = window_of(width)
    pieces = packed.shape[0] // (c_local * rows)

    barrier = pltpu.get_barrier_semaphore()
    for k in range(1, n_amp):
        pl.semaphore_signal(barrier, inc=1, device_id={"amp": lax.rem(me_a + k, n_amp)}, device_id_type=MESH)
    for k in range(1, n_int):
        pl.semaphore_signal(barrier, inc=1, device_id={"int": lax.rem(me_i + k, n_int)}, device_id_type=MESH)
    small = [
        pltpu.make_async_copy(sizes_hbm, sizes, local_sem.at[2]),
        pltpu.make_async_copy(irreps_hbm, irreps, local_sem.at[3]),
        pltpu.make_async_copy(amps_hbm, amps, local_sem.at[0]),
    ]
    for copy in small:
        copy.start()
    ints_in = pltpu.make_async_copy(ints_hbm, ints, local_sem.at[1])
    ints_in.start()

    for copy in small:
        copy.wait()
    padded = -(-width // LANES) * LANES
    for c in range(c_local):
        irrep = irreps[c]
        start, end = jnp.int32(0), jnp.int32(0)
        for g in range(sizes.shape[0]):
            size = sizes[g]
            start += jnp.where(g < irrep, size, 0)
            end += jnp.where(g <= irrep, size, 0)
        wide = jnp.pad(amps[c].astype(jnp.float32), ((0, 0), (0, padded - width)))
        column = lax.broadcasted_iota(jnp.int32, (rows, padded), 1)
        wide = jnp.where((column >= start) & (column < end), wide, 0.0)
        stack = jnp.concatenate([wide[:, p * LANES:(p + 1) * LANES] for p in range(pieces)], axis=0)
        packed[c * pieces * rows:(c + 1) * pieces * rows, :] = stack.astype(jnp.bfloat16)

    pl.semaphore_wait(barrier, n_amp + n_int - 2)
    sends = []
    for k in range(1, n_amp):
        copy = pltpu.make_async_remote_copy(
            src_ref=packed, dst_ref=gathered.at[me_a], send_sem=g_send.at[k], recv_sem=g_recv.at[me_a],
            device_id={"amp": lax.rem(me_a + k, n_amp)}, device_id_type=MESH)
        copy.start()
        sends.append(copy)
    gathered[me_a] = packed[...]
    ints_in.wait()
    for k in range(1, n_amp):
        source = lax.rem(me_a + n_amp - k, n_amp)
        pltpu.make_async_remote_copy(
            src_ref=packed, dst_ref=gathered.at[source], send_sem=g_send.at[k], recv_sem=g_recv.at[source],
            device_id={"amp": source}, device_id_type=MESH).wait_recv()

    pages = gathered[...].astype(jnp.float32)
    lhs = []
    for c in range(c_local):
        at = [(c * pieces + p) * rows for p in range(pieces)]
        cut = [pages[:, r:r + rows, :].reshape(n_amp * rows, LANES).astype(jnp.bfloat16) for r in at]
        lhs.append(jnp.concatenate(cut, axis=1)[:, :win])
    for h in range(chunks):
        total = None
        for c in range(c_local):
            block = ints[c, :, h * chunk:(h + 1) * chunk]
            term = jnp.dot(lhs[c], block, preferred_element_type=jnp.float32)
            total = term if total is None else total + term
        part[h] = total.reshape(n_int, out_rows, chunk)
        for k in range(1, n_int):
            to = lax.rem(me_i + k, n_int)
            copy = pltpu.make_async_remote_copy(
                src_ref=part.at[h, to], dst_ref=landed.at[h, me_i], send_sem=r_send.at[h, k],
                recv_sem=r_recv.at[h, me_i], device_id={"int": to}, device_id_type=MESH)
            copy.start()
            sends.append(copy)
    for h in range(chunks):
        total = part[h, me_i]
        for k in range(1, n_int):
            source = lax.rem(me_i + n_int - k, n_int)
            pltpu.make_async_remote_copy(
                src_ref=part.at[h, source], dst_ref=landed.at[h, source], send_sem=r_send.at[h, k],
                recv_sem=r_recv.at[h, source], device_id={"int": source}, device_id_type=MESH).wait_recv()
            total = total + landed[h, source]
        out_ref[:, h * chunk:(h + 1) * chunk] = total
    for copy in sends:
        copy.wait_send()


def solution(mesh):
    n_amp, n_int = mesh.shape["amp"], mesh.shape["int"]

    def body(amps, integrals, irrep_sizes, c_irreps):
        rows, c_local, width = amps.shape
        columns = integrals.shape[0]
        out_rows = n_amp * rows // n_int
        chunks = chunks_of(columns)
        pieces = -(-window_of(width) // LANES)
        page = (c_local * pieces * rows, LANES)
        parts = (chunks, n_int, out_rows, columns // chunks)
        return pl.pallas_call(
            functools.partial(kernel, n_amp, n_int),
            out_shape=jax.ShapeDtypeStruct((out_rows, columns), jnp.float32),
            in_specs=[
                pl.BlockSpec(memory_space=pl.ANY),
            ] * 4,
            out_specs=pl.BlockSpec(memory_space=pltpu.VMEM),
            scratch_shapes=[
                pltpu.SMEM(irrep_sizes.shape, jnp.int32),
                pltpu.SMEM(c_irreps.shape, jnp.int32),
                pltpu.VMEM((c_local, rows, width), jnp.bfloat16),
                pltpu.VMEM((c_local, width, columns), jnp.bfloat16),
                pltpu.VMEM(page, jnp.bfloat16),
                pltpu.VMEM((n_amp,) + page, jnp.bfloat16),
                pltpu.VMEM(parts, jnp.float32),
                pltpu.VMEM(parts, jnp.float32),
                pltpu.SemaphoreType.DMA((4,)),
                pltpu.SemaphoreType.DMA((n_amp,)),
                pltpu.SemaphoreType.DMA((n_amp,)),
                pltpu.SemaphoreType.DMA((chunks, n_int)),
                pltpu.SemaphoreType.DMA((chunks, n_int)),
            ],
            compiler_params=pltpu.CompilerParams(
                collective_id=0, has_side_effects=True, vmem_limit_bytes=63 * 1024 * 1024
            ),
            cost_estimate=pl.CostEstimate(
                flops=2 * n_amp * rows * columns * width, bytes_accessed=2 * columns * width, transcendentals=0
            ),
        )(irrep_sizes, c_irreps, jnp.transpose(amps, (1, 0, 2)), jnp.transpose(integrals, (1, 2, 0)))

    placed = (P("amp", "int", None), P("amp", "int", None), P(), P("int"))
    return jax.shard_map(
        body, mesh=mesh, in_specs=placed, out_specs=P("int", "amp"), check_vma=False
    )
```

time: 58.3 us -> 18.2 us (0.31)
  waiting for transfers between devices: 25.2 us -> 0 us
  Pallas kernels: 0 us -> 15.9 us
  blocking collectives: 15.7 us -> 0 us
  between operations: 14.2 us -> 0.66 us
  other arithmetic: 1.65 us -> 0 us
  local copies, waits for them, and re-layouts: 0.01 us -> 1.47 us
  matrix products: 1.25 us -> 0 us
    reduce_scatter x1 -> x0, waiting for transfers between devices: 25.2 us -> none  [body(): lax.psum_scatter(partial_sums, 'int', scatter_dimension=0, tiled=True)]
    pallas_call x0 -> x1, Pallas kernels: none -> 15.9 us  [body(): pl.pallas_call(functools.partial(kernel, n_amp, n_int), out_shape=jax.Sha...]
    all_gather x1 -> x0, blocking collectives: 15.7 us -> none  [body(): piece = lax.all_gather(blocked, 'amp', axis=0, tiled=True)]
    unnamed x2 -> x1, local copies, waits for them, and re-layouts: 0.01 us -> 1.47 us
    dot_general x1 -> x0, matrix products: 1.25 us -> none  [body(): lax.dot_general(rows, flat_ints, (((1,), (1,)), ((), ())), preferred_elem...]
    another operation x1 -> x0, other arithmetic: 0.83 us -> none
    mul x1 -> x0, other arithmetic: 0.73 us -> none  [body(): blocked = amps * allowed[None, :, :]]
  transfers between devices with their start and end apart: 1 -> 0, of which waited for: 1 -> 0; matrix products, arithmetic and copies ran while one was open for 0% -> 0% of each run, Pallas kernels for 0% -> 0%
where the time goes in v1:
time: 18.2 us; the launch traced here: 18 us
  Pallas kernels  15.9 us (87%)
  local copies, waits for them, and re-layouts  1.47 us (8%)
  between operations  0.66 us (4%)
    pallas_call x1, Pallas kernels, body(): pl.pallas_call(functools.partial(kernel, n_amp, n_int), out_shape=jax.Sha...  15.9 us
    unnamed x1, local copies, waits for them, and re-layouts  1.47 us

profile of v1, /device:TPU:0, one launch (start us, length us, event | category | flops | bytes accessed | tf_op | source)
XLA Modules:
  0.0 18.0 jit_solution(7700881830747072942)
XLA Ops:
  0.7 15.9 %shard_map.46 = f32[16,1024]{1,0:T(8,128)} custom-call(s32[8]{0:T(128)} %sizes_hbm.1, s32[1]{0:T(128)S(6)} %copy.6.irreps_hbm, bf16[1,8,1000]{2,1,0:T(8,128)(2,1)} %bitcast.3, bf16[1,1000,1024]{2,1,0:T(8,128)(2,1)} %bitcast.2), custom_call_target="tpu_custom_call" | custom-call | flops 131072000 | bytes 2048000 | tf_op jit(solution)/shard_map/pallas_call | solution.py:124
  16.5 1.5 %copy.7 = f32[16,1024]{1,0:T(8,128)} copy(f32[16,1024]{1,0:T(8,128)} %shard_map.46) | data formatting | bytes 131072

commit v2 on v1

--- a/solution.py
+++ b/solution.py
@@ -13,21 +13,42 @@
 LANES = 128
 
 
-def window_of(width):
-    return width
+def tiles_of(width):
+    tiles = -(-width // TILE)
+    return tiles, min(tiles, -(-(MOST + TILE - 1) // TILE))
+
+
+def levels_of(last):
+    levels = []
+    while sum(levels) < last:
+        levels.insert(0, 2 * levels[0] if levels else 1)
+    return levels
+
+
+def shifted(parts, kept, levels, first):
+    for i, step in enumerate(levels):
+        need = kept + sum(levels[i + 1:])
+        odd = lax.rem(lax.div(first, step), 2) == 1
+        parts = [
+            jnp.where(odd, parts[j + step], parts[j]) if j + step < len(parts) else parts[j]
+            for j in range(min(need, len(parts)))
+        ]
+    return parts
 
 
 def chunks_of(columns):
     return 4 if columns % (4 * LANES) == 0 else 1
 
 
-def kernel(n_amp, n_int, sizes_hbm, irreps_hbm, amps_hbm, ints_hbm, out_ref, sizes, irreps, amps, ints, packed, gathered, part, landed,
+def kernel(n_amp, n_int, sizes_hbm, irreps_hbm, amps_hbm, ints_hbm, out_ref, sizes, irreps, amps, ints, window, packed, gathered, part, landed,
            local_sem, g_send, g_recv, r_send, r_recv):
     me_a, me_i = lax.axis_index("amp"), lax.axis_index("int")
     c_local, rows, width = amps.shape
     columns = ints.shape[2]
     chunks, _, out_rows, chunk = part.shape
-    win = window_of(width)
+    tiles, kept = tiles_of(width)
+    levels = levels_of(tiles - kept)
+    win = kept * TILE
     pieces = packed.shape[0] // (c_local * rows)
 
     barrier = pltpu.get_barrier_semaphore()
@@ -45,6 +66,7 @@
     ints_in = pltpu.make_async_copy(ints_hbm, ints, local_sem.at[1])
     ints_in.start()
 
+    firsts = []
     for copy in small:
         copy.wait()
     padded = -(-width // LANES) * LANES
@@ -55,9 +77,14 @@
             size = sizes[g]
             start += jnp.where(g < irrep, size, 0)
             end += jnp.where(g <= irrep, size, 0)
+        first = jnp.minimum(lax.div(start, TILE), tiles - kept)
+        firsts.append(first)
         wide = jnp.pad(amps[c].astype(jnp.float32), ((0, 0), (0, padded - width)))
         column = lax.broadcasted_iota(jnp.int32, (rows, padded), 1)
         wide = jnp.where((column >= start) & (column < end), wide, 0.0)
+        for step in levels:
+            odd = lax.rem(lax.div(first, step), 2) == 1
+            wide = jnp.where(odd, pltpu.roll(wide, padded - step * TILE, 1), wide)
         stack = jnp.concatenate([wide[:, p * LANES:(p + 1) * LANES] for p in range(pieces)], axis=0)
         packed[c * pieces * rows:(c + 1) * pieces * rows, :] = stack.astype(jnp.bfloat16)
 
@@ -71,6 +98,16 @@
         sends.append(copy)
     gathered[me_a] = packed[...]
     ints_in.wait()
+    for c in range(c_local):
+        for l in range(0, columns, LANES):
+            lanes = slice(l, l + LANES)
+            block = [ints[c, t * TILE:(t + 1) * TILE, lanes] for t in range(width // TILE)]
+            if width % TILE:
+                rest = ints[c, width // TILE * TILE:, lanes].astype(jnp.float32)
+                rest = jnp.concatenate([rest, jnp.zeros((TILE - width % TILE, LANES), jnp.float32)], axis=0)
+                block.append(rest.astype(jnp.bfloat16))
+            for t, tile in enumerate(shifted(block, kept, levels, firsts[c])):
+                window[c, t * TILE:(t + 1) * TILE, lanes] = tile
     for k in range(1, n_amp):
         source = lax.rem(me_a + n_amp - k, n_amp)
         pltpu.make_async_remote_copy(
@@ -86,7 +123,7 @@
     for h in range(chunks):
         total = None
         for c in range(c_local):
-            block = ints[c, :, h * chunk:(h + 1) * chunk]
+            block = window[c, :, h * chunk:(h + 1) * chunk]
             term = jnp.dot(lhs[c], block, preferred_element_type=jnp.float32)
             total = term if total is None else total + term
         part[h] = total.reshape(n_int, out_rows, chunk)
@@ -118,7 +155,8 @@
         columns = integrals.shape[0]
         out_rows = n_amp * rows // n_int
         chunks = chunks_of(columns)
-        pieces = -(-window_of(width) // LANES)
+        win = tiles_of(width)[1] * TILE
+        pieces = -(-win // LANES)
         page = (c_local * pieces * rows, LANES)
         parts = (chunks, n_int, out_rows, columns // chunks)
         return pl.pallas_call(
@@ -133,6 +171,7 @@
                 pltpu.SMEM(c_irreps.shape, jnp.int32),
                 pltpu.VMEM((c_local, rows, width), jnp.bfloat16),
                 pltpu.VMEM((c_local, width, columns), jnp.bfloat16),
+                pltpu.VMEM((c_local, win, columns), jnp.bfloat16),
                 pltpu.VMEM(page, jnp.bfloat16),
                 pltpu.VMEM((n_amp,) + page, jnp.bfloat16),
                 pltpu.VMEM(parts, jnp.float32),

time: 18.2 us -> 17.3 us (0.951)
  Pallas kernels: 15.9 us -> 15 us
    pallas_call x1, Pallas kernels: 15.9 us -> 15 us  [body(): pl.pallas_call(functools.partial(kernel, n_amp, n_int), out_shape=jax.Sha...]
where the time goes in v2:
time: 17.3 us; the launch traced here: 17.2 us
  Pallas kernels  15 us (87%)
  local copies, waits for them, and re-layouts  1.47 us (8%)
  between operations  0.66 us (4%)
    pallas_call x1, Pallas kernels, body(): pl.pallas_call(functools.partial(kernel, n_amp, n_int), out_shape=jax.Sha...  15 us
    unnamed x1, local copies, waits for them, and re-layouts  1.47 us

profile of v2, /device:TPU:0, one launch (start us, length us, event | category | flops | bytes accessed | tf_op | source)
XLA Modules:
  0.0 17.2 jit_solution(13281074564204693302)
XLA Ops:
  0.7 15.0 %shard_map.46 = f32[16,1024]{1,0:T(8,128)} custom-call(s32[8]{0:T(128)} %sizes_hbm.1, s32[1]{0:T(128)S(6)} %copy.6.irreps_hbm, bf16[1,8,1000]{2,1,0:T(8,128)(2,1)} %bitcast.3, bf16[1,1000,1024]{2,1,0:T(8,128)(2,1)} %bitcast.2), custom_call_target="tpu_custom_call" | custom-call | flops 131072000 | bytes 2048000 | tf_op jit(solution)/shard_map/pallas_call | solution.py:162
  15.7 1.5 %copy.7 = f32[16,1024]{1,0:T(8,128)} copy(f32[16,1024]{1,0:T(8,128)} %shard_map.46) | data formatting | bytes 131072

commit v3 on v2

--- a/solution.py
+++ b/solution.py
@@ -40,7 +40,7 @@
     return 4 if columns % (4 * LANES) == 0 else 1
 
 
-def kernel(n_amp, n_int, sizes_hbm, irreps_hbm, amps_hbm, ints_hbm, out_ref, sizes, irreps, amps, ints, window, packed, gathered, part, landed,
+def kernel(n_amp, n_int, sizes_hbm, irreps, amps_hbm, ints_hbm, out_hbm, sizes, amps, ints, window, packed, gathered, part,
            local_sem, g_send, g_recv, r_send, r_recv):
     me_a, me_i = lax.axis_index("amp"), lax.axis_index("int")
     c_local, rows, width = amps.shape
@@ -58,7 +58,6 @@
         pl.semaphore_signal(barrier, inc=1, device_id={"int": lax.rem(me_i + k, n_int)}, device_id_type=MESH)
     small = [
         pltpu.make_async_copy(sizes_hbm, sizes, local_sem.at[2]),
-        pltpu.make_async_copy(irreps_hbm, irreps, local_sem.at[3]),
         pltpu.make_async_copy(amps_hbm, amps, local_sem.at[0]),
     ]
     for copy in small:
@@ -120,6 +119,7 @@
         at = [(c * pieces + p) * rows for p in range(pieces)]
         cut = [pages[:, r:r + rows, :].reshape(n_amp * rows, LANES).astype(jnp.bfloat16) for r in at]
         lhs.append(jnp.concatenate(cut, axis=1)[:, :win])
+    kept_here = []
     for h in range(chunks):
         total = None
         for c in range(c_local):
@@ -130,19 +130,23 @@
         for k in range(1, n_int):
             to = lax.rem(me_i + k, n_int)
             copy = pltpu.make_async_remote_copy(
-                src_ref=part.at[h, to], dst_ref=landed.at[h, me_i], send_sem=r_send.at[h, k],
+                src_ref=part.at[h, to], dst_ref=out_hbm.at[me_i, :, h * chunk:(h + 1) * chunk], send_sem=r_send.at[h, k],
                 recv_sem=r_recv.at[h, me_i], device_id={"int": to}, device_id_type=MESH)
             copy.start()
             sends.append(copy)
+        copy = pltpu.make_async_copy(
+            part.at[h, me_i], out_hbm.at[me_i, :, h * chunk:(h + 1) * chunk], r_recv.at[h, me_i])
+        copy.start()
+        kept_here.append(copy)
     for h in range(chunks):
-        total = part[h, me_i]
         for k in range(1, n_int):
             source = lax.rem(me_i + n_int - k, n_int)
             pltpu.make_async_remote_copy(
-                src_ref=part.at[h, source], dst_ref=landed.at[h, source], send_sem=r_send.at[h, k],
-                recv_sem=r_recv.at[h, source], device_id={"int": source}, device_id_type=MESH).wait_recv()
-            total = total + landed[h, source]
-        out_ref[:, h * chunk:(h + 1) * chunk] = total
+                src_ref=part.at[h, source], dst_ref=out_hbm.at[source, :, h * chunk:(h + 1) * chunk],
+                send_sem=r_send.at[h, k], recv_sem=r_recv.at[h, source], device_id={"int": source},
+                device_id_type=MESH).wait_recv()
+    for copy in kept_here:
+        copy.wait()
     for copy in sends:
         copy.wait_send()
 
@@ -159,24 +163,25 @@
         pieces = -(-win // LANES)
         page = (c_local * pieces * rows, LANES)
         parts = (chunks, n_int, out_rows, columns // chunks)
-        return pl.pallas_call(
+        addends = pl.pallas_call(
             functools.partial(kernel, n_amp, n_int),
-            out_shape=jax.ShapeDtypeStruct((out_rows, columns), jnp.float32),
+            out_shape=jax.ShapeDtypeStruct((n_int, out_rows, columns), jnp.float32),
             in_specs=[
                 pl.BlockSpec(memory_space=pl.ANY),
-            ] * 4,
-            out_specs=pl.BlockSpec(memory_space=pltpu.VMEM),
+                pl.BlockSpec(memory_space=pltpu.SMEM),
+                pl.BlockSpec(memory_space=pl.ANY),
+                pl.BlockSpec(memory_space=pl.ANY),
+            ],
+            out_specs=pl.BlockSpec(memory_space=pl.ANY),
             scratch_shapes=[
                 pltpu.SMEM(irrep_sizes.shape, jnp.int32),
-                pltpu.SMEM(c_irreps.shape, jnp.int32),
                 pltpu.VMEM((c_local, rows, width), jnp.bfloat16),
                 pltpu.VMEM((c_local, width, columns), jnp.bfloat16),
                 pltpu.VMEM((c_local, win, columns), jnp.bfloat16),
                 pltpu.VMEM(page, jnp.bfloat16),
                 pltpu.VMEM((n_amp,) + page, jnp.bfloat16),
                 pltpu.VMEM(parts, jnp.float32),
-                pltpu.VMEM(parts, jnp.float32),
-                pltpu.SemaphoreType.DMA((4,)),
+                pltpu.SemaphoreType.DMA((3,)),
                 pltpu.SemaphoreType.DMA((n_amp,)),
                 pltpu.SemaphoreType.DMA((n_amp,)),
                 pltpu.SemaphoreType.DMA((chunks, n_int)),
@@ -189,6 +194,7 @@
                 flops=2 * n_amp * rows * columns * width, bytes_accessed=2 * columns * width, transcendentals=0
             ),
         )(irrep_sizes, c_irreps, jnp.transpose(amps, (1, 0, 2)), jnp.transpose(integrals, (1, 2, 0)))
+        return jnp.sum(addends, axis=0)
 
     placed = (P("amp", "int", None), P("amp", "int", None), P(), P("int"))
     return jax.shard_map(

time: 17.3 us -> 16.9 us (0.977)
  other arithmetic: 0 us -> 1.6 us
  local copies, waits for them, and re-layouts: 1.47 us -> 0 us
  Pallas kernels: 15 us -> 14.5 us
    reduce_sum x0 -> x1, other arithmetic: none -> 1.6 us  [body(): return jnp.sum(addends, axis=0)]
    unnamed x1 -> x0, local copies, waits for them, and re-layouts: 1.47 us -> none
    pallas_call x1, Pallas kernels: 15 us -> 14.5 us  [body(): pl.pallas_call(functools.partial(kernel, n_amp, n_int), out_shape=jax.Sha...]
where the time goes in v3:
time: 16.9 us; the launch traced here: 16.8 us
  Pallas kernels  14.5 us (86%)
  other arithmetic  1.6 us (9%)
  between operations  0.66 us (4%)
    pallas_call x1, Pallas kernels, body(): pl.pallas_call(functools.partial(kernel, n_amp, n_int), out_shape=jax.Sha...  14.5 us
    reduce_sum x1, other arithmetic, body(): return jnp.sum(addends, axis=0)  1.6 us

profile of v3, /device:TPU:0, one launch (start us, length us, event | category | flops | bytes accessed | tf_op | source)
XLA Modules:
  0.0 16.8 jit_solution(12004234747225518347)
XLA Ops:
  0.7 14.5 %shard_map.46 = f32[4,16,1024]{2,1,0:T(8,128)} custom-call(s32[8]{0:T(128)} %sizes_hbm.1, s32[1]{0:T(128)S(6)} %copy.5.irreps, bf16[1,8,1000]{2,1,0:T(8,128)(2,1)} %bitcast.3, bf16[1,1000,1024]{2,1,0:T(8,128)(2,1)} %bitcast.2), custom_call_target="tpu_custom_call" | custom-call | flops 131072000 | bytes 2048000 | tf_op jit(solution)/shard_map/pallas_call | solution.py:166
  15.2 1.6 %reduce_sum.9 = f32[16,1024]{1,0:T(8,128)} reduce(f32[4,16,1024]{2,1,0:T(8,128)} %shard_map.46, f32[]{:T(128)} %constant.0.clone.1), dimensions={0}, to_apply=%region_0.0 | reduce | flops 49152 | bytes 327684 | tf_op jit(solution)/shard_map/reduce_sum | solution.py:197

commit v4 on v2

--- a/solution.py
+++ b/solution.py
@@ -37,15 +37,19 @@
 
 
 def chunks_of(columns):
-    return 4 if columns % (4 * LANES) == 0 else 1
-
-
-def kernel(n_amp, n_int, sizes_hbm, irreps_hbm, amps_hbm, ints_hbm, out_ref, sizes, irreps, amps, ints, window, packed, gathered, part, landed,
+    return 2 if columns % (2 * LANES) == 0 else 1
+
+
+def step_of(grade):
+    return jnp.exp2(grade * (1.0 / 64.0) - 15.0)
+
+
+def kernel(n_amp, n_int, sizes_hbm, irreps, amps_hbm, ints_hbm, out_ref, sizes, amps, ints, window, packed, gathered, exact, part, landed,
            local_sem, g_send, g_recv, r_send, r_recv):
     me_a, me_i = lax.axis_index("amp"), lax.axis_index("int")
     c_local, rows, width = amps.shape
     columns = ints.shape[2]
-    chunks, _, out_rows, chunk = part.shape
+    chunks, _, out_rows, chunk = exact.shape
     tiles, kept = tiles_of(width)
     levels = levels_of(tiles - kept)
     win = kept * TILE
@@ -58,7 +62,6 @@
         pl.semaphore_signal(barrier, inc=1, device_id={"int": lax.rem(me_i + k, n_int)}, device_id_type=MESH)
     small = [
         pltpu.make_async_copy(sizes_hbm, sizes, local_sem.at[2]),
-        pltpu.make_async_copy(irreps_hbm, irreps, local_sem.at[3]),
         pltpu.make_async_copy(amps_hbm, amps, local_sem.at[0]),
     ]
     for copy in small:
@@ -126,7 +129,14 @@
             block = window[c, :, h * chunk:(h + 1) * chunk]
             term = jnp.dot(lhs[c], block, preferred_element_type=jnp.float32)
             total = term if total is None else total + term
-        part[h] = total.reshape(n_int, out_rows, chunk)
+        exact[h] = total.reshape(n_int, out_rows, chunk)
+        top = jnp.max(jnp.abs(total), axis=1, keepdims=True)
+        grade = jnp.ceil(jnp.log2(jnp.maximum(top, 2.0 ** -100)) * 64.0) + 1.0
+        whole = jnp.floor(total * (1.0 / step_of(grade)) + 0.5)
+        whole = jnp.minimum(jnp.maximum(whole, -32767.0), 32767.0)
+        coded = jnp.concatenate([whole, jnp.broadcast_to(grade, (grade.shape[0], LANES))], axis=1)
+        coded = coded.astype(jnp.int32).astype(jnp.int16)
+        part[h] = coded.reshape(n_int, out_rows, chunk + LANES)
         for k in range(1, n_int):
             to = lax.rem(me_i + k, n_int)
             copy = pltpu.make_async_remote_copy(
@@ -135,13 +145,15 @@
             copy.start()
             sends.append(copy)
     for h in range(chunks):
-        total = part[h, me_i]
+        total = exact[h, me_i]
         for k in range(1, n_int):
             source = lax.rem(me_i + n_int - k, n_int)
             pltpu.make_async_remote_copy(
                 src_ref=part.at[h, source], dst_ref=landed.at[h, source], send_sem=r_send.at[h, k],
                 recv_sem=r_recv.at[h, source], device_id={"int": source}, device_id_type=MESH).wait_recv()
-            total = total + landed[h, source]
+            coded = landed[h, source].astype(jnp.int32).astype(jnp.float32)
+            step = step_of(coded[:, chunk:])
+            total = total + coded[:, :chunk] * jnp.concatenate([step] * (chunk // LANES), axis=1)
         out_ref[:, h * chunk:(h + 1) * chunk] = total
     for copy in sends:
         copy.wait_send()
@@ -159,24 +171,28 @@
         pieces = -(-win // LANES)
         page = (c_local * pieces * rows, LANES)
         parts = (chunks, n_int, out_rows, columns // chunks)
+        coded = parts[:3] + (parts[3] + LANES,)
         return pl.pallas_call(
             functools.partial(kernel, n_amp, n_int),
             out_shape=jax.ShapeDtypeStruct((out_rows, columns), jnp.float32),
             in_specs=[
                 pl.BlockSpec(memory_space=pl.ANY),
-            ] * 4,
+                pl.BlockSpec(memory_space=pltpu.SMEM),
+                pl.BlockSpec(memory_space=pl.ANY),
+                pl.BlockSpec(memory_space=pl.ANY),
+            ],
             out_specs=pl.BlockSpec(memory_space=pltpu.VMEM),
             scratch_shapes=[
                 pltpu.SMEM(irrep_sizes.shape, jnp.int32),
-                pltpu.SMEM(c_irreps.shape, jnp.int32),
                 pltpu.VMEM((c_local, rows, width), jnp.bfloat16),
                 pltpu.VMEM((c_local, width, columns), jnp.bfloat16),
                 pltpu.VMEM((c_local, win, columns), jnp.bfloat16),
                 pltpu.VMEM(page, jnp.bfloat16),
                 pltpu.VMEM((n_amp,) + page, jnp.bfloat16),
                 pltpu.VMEM(parts, jnp.float32),
-                pltpu.VMEM(parts, jnp.float32),
-                pltpu.SemaphoreType.DMA((4,)),
+                pltpu.VMEM(coded, jnp.int16),
+                pltpu.VMEM(coded, jnp.int16),
+                pltpu.SemaphoreType.DMA((3,)),
                 pltpu.SemaphoreType.DMA((n_amp,)),
                 pltpu.SemaphoreType.DMA((n_amp,)),
                 pltpu.SemaphoreType.DMA((chunks, n_int)),

time: 17.3 us -> 16.3 us (0.942)
  Pallas kernels: 15 us -> 13.9 us
    pallas_call x1, Pallas kernels: 15 us -> 13.9 us  [body(): pl.pallas_call(functools.partial(kernel, n_amp, n_int), out_shape=jax.Sha...]
where the time goes in v4:
time: 16.3 us; the launch traced here: 16.1 us
  Pallas kernels  13.9 us (85%)
  local copies, waits for them, and re-layouts  1.47 us (9%)
  between operations  0.66 us (4%)
    pallas_call x1, Pallas kernels, body(): pl.pallas_call(functools.partial(kernel, n_amp, n_int), out_shape=jax.Sha...  13.9 us
    unnamed x1, local copies, waits for them, and re-layouts  1.47 us

profile of v4, /device:TPU:0, one launch (start us, length us, event | category | flops | bytes accessed | tf_op | source)
XLA Modules:
  0.0 16.1 jit_solution(12585969346721682891)
XLA Ops:
  0.7 13.9 %shard_map.46 = f32[16,1024]{1,0:T(8,128)} custom-call(s32[8]{0:T(128)} %sizes_hbm.1, s32[1]{0:T(128)S(6)} %copy.6.irreps, bf16[1,8,1000]{2,1,0:T(8,128)(2,1)} %bitcast.3, bf16[1,1000,1024]{2,1,0:T(8,128)(2,1)} %bitcast.2), custom_call_target="tpu_custom_call" | custom-call | flops 131072000 | bytes 2048000 | tf_op jit(solution)/shard_map/pallas_call | solution.py:175
  14.6 1.5 %copy.7 = f32[16,1024]{1,0:T(8,128)} copy(f32[16,1024]{1,0:T(8,128)} %shard_map.46) | data formatting | bytes 131072

commit v5 on v4

--- a/solution.py
+++ b/solution.py
@@ -37,7 +37,7 @@
 
 
 def chunks_of(columns):
-    return 2 if columns % (2 * LANES) == 0 else 1
+    return 1
 
 
 def step_of(grade):

time: 16.3 us -> 15.9 us (0.975)
  Pallas kernels: 13.9 us -> 13.6 us
    pallas_call x1, Pallas kernels: 13.9 us -> 13.6 us  [body(): pl.pallas_call(functools.partial(kernel, n_amp, n_int), out_shape=jax.Sha...]
where the time goes in v5:
time: 15.9 us; the launch traced here: 15.7 us
  Pallas kernels  13.6 us (86%)
  local copies, waits for them, and re-layouts  1.47 us (9%)
  between operations  0.66 us (4%)
    pallas_call x1, Pallas kernels, body(): pl.pallas_call(functools.partial(kernel, n_amp, n_int), out_shape=jax.Sha...  13.6 us
    unnamed x1, local copies, waits for them, and re-layouts  1.47 us

profile of v5, /device:TPU:0, one launch (start us, length us, event | category | flops | bytes accessed | tf_op | source)
XLA Modules:
  0.0 15.7 jit_solution(5706102596579787758)
XLA Ops:
  0.7 13.6 %shard_map.46 = f32[16,1024]{1,0:T(8,128)} custom-call(s32[8]{0:T(128)} %sizes_hbm.1, s32[1]{0:T(128)S(6)} %copy.6.irreps, bf16[1,8,1000]{2,1,0:T(8,128)(2,1)} %bitcast.3, bf16[1,1000,1024]{2,1,0:T(8,128)(2,1)} %bitcast.2), custom_call_target="tpu_custom_call" | custom-call | flops 131072000 | bytes 2048000 | tf_op jit(solution)/shard_map/pallas_call | solution.py:175
  14.3 1.5 %copy.7 = f32[16,1024]{1,0:T(8,128)} copy(f32[16,1024]{1,0:T(8,128)} %shard_map.46) | data formatting | bytes 131072
